TPU v7x, 512 devices: a whole 4x4x16 slice. The times are simulated.
512 devices in a mesh: serve: 64 (over y, z), head: 8 (over x, core).
Axes of the slice: x: 4, y: 4, z: 16, core: 2. Of those that a mesh axis runs over, the one named last changes fastest.
Arguments:
- queries: bfloat16 [2, 2048, 8192], P(None, ('serve', 'head')), may hold values from -5 to 5
- new_kv: bfloat16 [2, 2048, 2048], P(None, ('serve', 'head')), may hold values from -5 to 5
- suffix_kv: bfloat16 [2048, 8, 2, 128, 128], P('serve', 'head'), may hold values from -5 to 5
- prefix_kv: bfloat16 [128, 8, 2, 2048, 128], P('serve', 'head'), may hold values from -5 to 5
- owner_map: int32 [32, 2], replicated, may hold values from 0 to 127, as said below
- host_slot: int32 [2048], replicated, may hold values from 0 to 2047, as said below
- suffix_len: int32 [2048], replicated, may hold values from 1 to 128, 131072 in all
Outputs:
- attended: bfloat16 [2, 2048, 8192], P(None, ('serve', 'head'))
Inputs may be any that keep to these rules, and one draw needn't show every extreme that they name: `owner_map`: an entry is device * 2 + slot on the serve axis; no slot is named twice; the two halves of a prompt lie on different devices; 16 devices hold two slabs, 32 hold one and the rest none. `host_slot`: every slot holds one sample; the samples of every prompt are spread evenly, 1 to each serve device; slot g lies on serve device g // 32.
All inputs are finite; a program needn't handle non-finite values.
Results may differ from a plain program's by a relative error of at most 0.0047.
Values may be sent and summed in bfloat16 or wider, within the bound.
A program may use at most 64 MiB of HBM per device.

v0:
```python
import jax
import jax.numpy as jnp
from jax import lax
from jax.sharding import PartitionSpec as P

HD = 128
QH = 64
KVH = 8
SPP = 64
STEPS = 2
SLOTS = 2


def local(queries, new_kv, suffix_kv, prefix_kv, owner_map, host_slot, suffix_len):
    serve_count = lax.axis_size("serve")
    my_index = lax.axis_index("serve")
    host_count = suffix_kv.shape[0]
    group_count = suffix_kv.shape[1]
    suffix_cap = suffix_kv.shape[3]
    per_group = QH // KVH
    repeats = SPP // serve_count
    prompt_count = owner_map.shape[0]
    row_width = group_count * per_group * HD
    score_scale = HD ** (-0.5)
    query_local, fresh_local = (
        lax.all_to_all(queries, "head", split_axis=2, concat_axis=1, tiled=True),
        lax.all_to_all(new_kv, "head", split_axis=2, concat_axis=1, tiled=True),
    )
    host_device = (host_slot // host_count).reshape(prompt_count, SPP)
    host_within = (host_slot % host_count).reshape(prompt_count, SPP)
    present = host_device[None] == jnp.arange(serve_count, dtype=jnp.int32)[:, None, None]
    rank_table = jnp.cumsum(present.astype(jnp.int32), axis=2) - 1
    picked = present[..., None] & (rank_table[..., None] == jnp.arange(repeats, dtype=jnp.int32))
    local_table = jnp.sum(jnp.where(picked, host_within[None, :, :, None], 0), axis=2)
    slab_count = serve_count * SLOTS
    owner_flat = owner_map.reshape(-1)
    matched = owner_flat[None, :] == jnp.arange(slab_count, dtype=jnp.int32)[:, None]
    prompt_ids = jnp.arange(2 * prompt_count, dtype=jnp.int32) // 2
    slab_prompt = jnp.sum(jnp.where(matched, prompt_ids[None, :], 0), axis=1).reshape(
        serve_count, SLOTS
    )
    own_table = local_table[my_index]
    everyone = lax.all_gather(query_local, "serve", axis=1, tiled=True)
    wanted = jnp.take(local_table, slab_prompt[my_index], axis=1)
    row_index = wanted + (jnp.arange(serve_count, dtype=jnp.int32) * host_count)[:, None, None]
    incoming = jnp.take(everyone, row_index.reshape(-1), axis=1)
    arranged = incoming.reshape(STEPS, serve_count, SLOTS, repeats, group_count, per_group, HD)
    part_outs = []
    part_logs = []
    for slot_index in range(SLOTS):
        chosen = arranged[:, :, slot_index]
        scores = (
            jnp.einsum(
                "tnrcgd,ckd->tnrcgk",
                chosen,
                prefix_kv[slot_index, :, 0],
                preferred_element_type=jnp.float32,
            )
            * score_scale
        )
        maximum = jnp.max(scores, axis=-1, keepdims=True)
        exponent = jnp.exp(scores - maximum)
        totals = jnp.sum(exponent, axis=-1)
        weights = exponent.astype(jnp.bfloat16)
        blended = (
            jnp.einsum(
                "tnrcgk,ckd->tnrcgd",
                weights,
                prefix_kv[slot_index, :, 1],
                preferred_element_type=jnp.float32,
            )
            / totals[..., None]
        )
        part_outs.append(blended)
        part_logs.append(maximum[..., 0] + jnp.log(totals))
    stacked_out = jnp.stack(part_outs, axis=2).reshape(STEPS, slab_count * repeats, row_width)
    stacked_log = jnp.stack(part_logs, axis=2).reshape(
        STEPS, slab_count * repeats, group_count * per_group
    )
    back_out, back_log = (
        lax.all_to_all(stacked_out, "serve", split_axis=1, concat_axis=1, tiled=True),
        lax.all_to_all(stacked_log, "serve", split_axis=1, concat_axis=1, tiled=True),
    )
    flat_local = own_table.reshape(-1)
    slot_match = flat_local[None, :] == jnp.arange(host_count, dtype=jnp.int32)[:, None]
    position = jnp.sum(
        jnp.where(slot_match, jnp.arange(prompt_count * repeats, dtype=jnp.int32)[None, :], 0),
        axis=1,
    )
    prompt_of = position // repeats
    rank_of = position % repeats
    half_index = (jnp.take(owner_map, prompt_of, axis=0) * repeats + rank_of[:, None]).reshape(-1)
    half_out = jnp.take(back_out, half_index, axis=1).reshape(
        STEPS, host_count, 2, group_count, per_group, HD
    )
    half_log = jnp.take(back_log, half_index, axis=1).reshape(
        STEPS, host_count, 2, group_count, per_group
    )
    my_slots = my_index * host_count + jnp.arange(host_count, dtype=jnp.int32)
    sample_hit = host_slot[None, :] == my_slots[:, None]
    lengths = jnp.sum(jnp.where(sample_hit, suffix_len[None, :], 0), axis=1)
    query_heads = query_local.reshape(STEPS, host_count, group_count, per_group, HD)
    fresh_pairs = fresh_local.reshape(STEPS, host_count, group_count, 2, HD)
    cache_scores = (
        jnp.einsum(
            "tkcgd,kcsd->tkcgs", query_heads, suffix_kv[:, :, 0], preferred_element_type=jnp.float32
        )
        * score_scale
    )
    cache_live = jnp.arange(suffix_cap, dtype=jnp.int32)[None, :] < lengths[:, None]
    cache_scores = jnp.where(cache_live[None, :, None, None, :], cache_scores, -jnp.inf)
    fresh_scores = (
        jnp.einsum(
            "tkcgd,ukcd->tkcgu",
            query_heads,
            fresh_pairs[:, :, :, 0],
            preferred_element_type=jnp.float32,
        )
        * score_scale
    )
    fresh_live = (
        jnp.arange(STEPS, dtype=jnp.int32)[None, :] <= jnp.arange(STEPS, dtype=jnp.int32)[:, None]
    )
    fresh_scores = jnp.where(fresh_live[:, None, None, None, :], fresh_scores, -jnp.inf)
    maximum = jnp.maximum(
        jnp.max(cache_scores, axis=-1, keepdims=True), jnp.max(fresh_scores, axis=-1, keepdims=True)
    )
    cache_exp = jnp.exp(cache_scores - maximum)
    fresh_exp = jnp.exp(fresh_scores - maximum)
    totals = jnp.sum(cache_exp, axis=-1) + jnp.sum(fresh_exp, axis=-1)
    own_sum = jnp.einsum(
        "tkcgs,kcsd->tkcgd",
        cache_exp.astype(jnp.bfloat16),
        suffix_kv[:, :, 1],
        preferred_element_type=jnp.float32,
    )
    own_sum = own_sum + jnp.einsum(
        "tkcgu,ukcd->tkcgd",
        fresh_exp.astype(jnp.bfloat16),
        fresh_pairs[:, :, :, 1],
        preferred_element_type=jnp.float32,
    )
    own_out = own_sum / totals[..., None]
    own_log = maximum[..., 0] + jnp.log(totals)
    highest = jnp.maximum(jnp.max(half_log, axis=2), own_log)
    half_factor = jnp.exp(half_log - highest[:, :, None])
    own_factor = jnp.exp(own_log - highest)
    numerator = jnp.sum(half_factor[..., None] * half_out, axis=2) + own_factor[..., None] * own_out
    denominator = jnp.sum(half_factor, axis=2) + own_factor
    attended = (
        (numerator / denominator[..., None])
        .astype(jnp.bfloat16)
        .reshape(STEPS, host_count, row_width)
    )
    return lax.all_to_all(attended, "head", split_axis=1, concat_axis=2, tiled=True)


def solution(mesh):
    return jax.shard_map(
        local,
        mesh=mesh,
        in_specs=(
            P(None, ("serve", "head"), None),
            P(None, ("serve", "head"), None),
            P("serve", "head", None, None, None),
            P("serve", "head", None, None, None),
            P(),
            P(),
            P(),
        ),
        out_specs=P(None, ("serve", "head"), None),
        check_vma=False,
    )
```

profile of v0, /device:TPU:1, one launch (start us, length us, event | category | flops | bytes accessed | tf_op | source)
XLA Modules:
  0.0 325.1 jit_solution(180073139882280549)
XLA Ops:
  6.5 8.4 %copy.98 = bf16[2,4,8192]{1,0,2:T(2,128)(2,1)} copy(bf16[2,4,8192]{2,1,0:T(4,128)(2,1)} %param.7) | data formatting | bytes 262144 | tf_op args[0]
  14.9 8.7 %reshape.643 = bf16[8,2,4096]{2,1,0:T(2,128)(2,1)S(1)} reshape(bf16[8192,2,4]{2,1,0:T(2,128)(2,1)} %bitcast.279) | data formatting | bytes 262144
  23.6 14.5 %all_to_all.61 = bf16[8,2,4096]{2,1,0:T(2,128)(2,1)S(1)} all-to-all(bf16[8,2,4096]{2,1,0:T(2,128)(2,1)S(1)} %reshape.643), channel_id=1, replica_groups=mesh['serve'=64,'head'=8] {'head'}, dimensions={0} | all-to-all | bytes 262144 | tf_op jit(solution)/shard_map/all_to_all | solution.py:26
  38.2 10.0 %reshape.644 = bf16[8192,2,4]{2,1,0:T(2,128)(2,1)} reshape(bf16[8,2,4096]{2,1,0:T(2,128)(2,1)S(1)} %all_to_all.61) | data formatting | bytes 262144
  48.2 10.7 %copy.99 = bf16[2,4,8,1024]{3,0,1,2:T(2,128)(2,1)} copy(bf16[2,4,8,1024]{1,0,3,2:T(2,128)(2,1)} %bitcast.278) | data formatting | bytes 262144 | tf_op jit(solution)/shard_map/all_to_all | solution.py:26
  58.9 0.9 copy.107
  59.8 2.6 reshape.645
  62.4 4.1 %all-to-all-start.2 = ((bf16[8,2,1024]{2,1,0:T(2,128)(2,1)}), bf16[8,2,1024]{2,1,0:T(2,128)(2,1)S(1)}, u32[]{:S(2)}, u32[]{:S(2)}) async-start(bf16[8,2,1024]{2,1,0:T(2,128)(2,1)} %reshape.645), calls=%async_computation.2 | async-start | bytes 65536 | tf_op jit(solution)/shard_map/all_to_all | solution.py:27
  67.2 0.1 broadcast_in_dim.174
  67.4 0.1 add.268
  67.7 14.4 %reduce_window_sum.11 = s32[64,32,64]{2,1,0:T(8,128)S(1)} reduce-window(s32[64,32,64]{2,1,0:T(8,128)S(1)} %fusion.35, s32[]{:T(128)} %constant.138.clone.1), window={size=1x1x64 pad=0_0x0_0x63_0}, to_apply=%region_0.1 | reduce-window | flops 8257536 | bytes 1048580 | tf_op jit(solution)/shard_map/jit(cumsum)/reduce_window_sum | solution.py:32
  82.1 1.2 select_reduce_fusion
  83.4 0.6 gather_fusion.1
  84.3 123.4 %all-gather.2.cloned.1.call-done = bf16[2,2048,1024]{2,0,1:T(2,128)(2,1)} async-done(((bf16[2,32,1024]{2,0,1:T(2,128)(2,1)}), bf16[2,2048,1024]{2,0,1:T(2,128)(2,1)}) %all-gather.2.cloned.1.call-update) | async-done | bytes 8388624 | tf_op jit(solution)/shard_map/all_gather | solution.py:43
  207.7 5.0 %gather_fusion.2 = bf16[128,2,1024]{2,1,0:T(2,128)(2,1)S(1)} fusion(bf16[2,2048,1024]{2,0,1:T(2,128)(2,1)} %all-gather.2.cloned.1.call-done, s32[1024]{0:T(1024)S(1)} %pad_clamp_fusion.1), kind=kCustom, calls=%fused_computation.2 | custom fusion | bytes 1049088 | tf_op jit(solution)/shard_map/jit(_take)/gather | solution.py:46
  212.7 0.3 reshape.641
  213.0 0.2 copy_select_fusion
  213.2 2.4 bitcast_reduce_fusion
  215.6 1.3 bitcast_reduce_fusion.1
  217.0 1.6 fusion.5
  218.6 1.5 fusion.45
  220.1 1.6 fusion.3
  221.7 1.5 fusion.39
  223.4 0.7 copy.105
  224.1 8.8 %all-to-all-start.1 = ((f32[2,128,8]{2,0,1:T(2,128)}), f32[2,128,8]{2,0,1:T(2,128)S(1)}, u32[]{:S(2)}, u32[]{:S(2)}) async-start(f32[2,128,8]{2,0,1:T(2,128)} %copy.105), calls=%async_computation.1 | async-start | bytes 262144 | tf_op jit(solution)/shard_map/all_to_all | solution.py:82
  233.2 1.5 reshape.642
  234.7 12.2 %all-to-all-done.1 = f32[2,128,8]{2,0,1:T(2,128)S(1)} async-done(((f32[2,128,8]{2,0,1:T(2,128)}), f32[2,128,8]{2,0,1:T(2,128)S(1)}, u32[]{:S(2)}, u32[]{:S(2)}) %all-to-all-start.1) | async-done | bytes 8224 | tf_op jit(solution)/shard_map/all_to_all | solution.py:82
  246.9 5.2 %all-to-all-start.3 = ((f32[2,128,1024]{2,0,1:T(2,128)}), f32[2,128,1024]{2,0,1:T(2,128)S(1)}, u32[]{:S(2)}, u32[]{:S(2)}) async-start(f32[2,128,1024]{2,0,1:T(2,128)} %reshape.642), calls=%async_computation.3 | async-start | bytes 2097152 | tf_op jit(solution)/shard_map/all_to_all | solution.py:81
  252.3 0.6 gather_fusion
  253.1 0.2 select_reduce_fusion.1
  253.4 2.2 reshape.646
  255.6 0.8 copy.108
  256.6 0.7 fusion.81
  257.3 2.0 fusion.80
  259.3 0.1 fusion.65
  259.5 0.3 fusion.59
  259.7 1.7 fusion.29
  261.4 0.7 gather_fusion.3
  262.1 0.2 fusion.63
  262.3 0.2 exponential_reduce_fusion
  262.4 0.1 subtract_exponential_fusion.1
  262.6 32.3 %all-to-all-done.3 = f32[2,128,1024]{2,0,1:T(2,128)S(1)} async-done(((f32[2,128,1024]{2,0,1:T(2,128)}), f32[2,128,1024]{2,0,1:T(2,128)S(1)}, u32[]{:S(2)}, u32[]{:S(2)}) %all-to-all-start.3) | async-done | bytes 1048608 | tf_op jit(solution)/shard_map/all_to_all | solution.py:81
  295.0 1.1 gather_fusion.4
  296.1 0.4 gather.42
  296.5 0.3 multiply_reduce_fusion
  296.8 0.4 fusion.28
  297.2 20.2 %all_to_all.62 = bf16[2,32,1024]{2,0,1:T(2,128)(2,1)S(1)} all-to-all(bf16[2,32,1024]{2,0,1:T(2,128)(2,1)S(1)} %reshape.587), channel_id=1, replica_groups=mesh['serve'=64,'head'=8] {'head'}, dimensions={1} | all-to-all | bytes 262144 | tf_op jit(solution)/shard_map/all_to_all | solution.py:155
  317.5 0.7 all_to_all.55
  (61 shorter events, 2.4 us)
Async XLA Ops:
  6.5 52.4 %copy-start.2 = (bf16[2,4,2048]{2,1,0:T(4,128)(2,1)S(1)}, bf16[2,4,2048]{2,1,0:T(4,128)(2,1)}, u32[]{:S(2)}) copy-start(bf16[2,4,2048]{2,1,0:T(4,128)(2,1)} %param.8) | copy-start | bytes 98308
  6.5 201.1 %all-gather.2.cloned.1.call-start = ((), (), s32[]{:S(2)}) async-start(), calls=%async_computation.5 | async-start | bytes 8519680 | tf_op jit(solution)/shard_map/all_gather | solution.py:43
  14.9 51.6 %copy-start.5 = (s32[32,2]{0,1:T(2,128)S(1)}, s32[32,2]{0,1:T(2,128)}, u32[]{:S(2)}) copy-start(s32[32,2]{0,1:T(2,128)} %param.11) | copy-start | bytes 772
  14.9 51.8 %copy-start.3 = (s32[2048]{0:T(1024)S(1)}, s32[2048]{0:T(1024)}, u32[]{:S(2)}) copy-start(s32[2048]{0:T(1024)} %param.12) | copy-start | bytes 24580
  62.4 161.7 %all-to-all-start.2 = ((bf16[8,2,1024]{2,1,0:T(2,128)(2,1)}), bf16[8,2,1024]{2,1,0:T(2,128)(2,1)S(1)}, u32[]{:S(2)}, u32[]{:S(2)}) async-start(bf16[8,2,1024]{2,1,0:T(2,128)(2,1)} %reshape.645), calls=%async_computation.2 | async-start | bytes 65536 | tf_op jit(solution)/shard_map/all_to_all | solution.py:27
  82.1 133.5 %copy-start.1 = (bf16[2,1,2,2048,128]{4,3,2,1,0:T(8,128)(2,1)S(1)}, bf16[2,1,2,2048,128]{4,3,2,1,0:T(8,128)(2,1)}, u32[]{:S(2)}) copy-start(bf16[2,1,2,2048,128]{4,3,2,1,0:T(8,128)(2,1)} %param.10) | copy-start | bytes 6291460
  221.7 31.4 %copy-start.4 = (s32[2048]{0:T(1024)S(1)}, s32[2048]{0:T(1024)}, u32[]{:S(2)}) copy-start(s32[2048]{0:T(1024)} %param.13) | copy-start | bytes 24580
  223.2 33.3 %copy-start = (bf16[2,4,8,1024]{3,0,1,2:T(2,128)(2,1)S(1)}, bf16[2,4,8,1024]{3,0,1,2:T(2,128)(2,1)}, u32[]{:S(2)}) copy-start(bf16[2,4,8,1024]{3,0,1,2:T(2,128)(2,1)} %copy.99) | copy-start | bytes 393220
  224.1 22.8 %all-to-all-start.1 = ((f32[2,128,8]{2,0,1:T(2,128)}), f32[2,128,8]{2,0,1:T(2,128)S(1)}, u32[]{:S(2)}, u32[]{:S(2)}) async-start(f32[2,128,8]{2,0,1:T(2,128)} %copy.105), calls=%async_computation.1 | async-start | bytes 262144 | tf_op jit(solution)/shard_map/all_to_all | solution.py:82
  246.9 48.0 %all-to-all-start.3 = ((f32[2,128,1024]{2,0,1:T(2,128)}), f32[2,128,1024]{2,0,1:T(2,128)S(1)}, u32[]{:S(2)}, u32[]{:S(2)}) async-start(f32[2,128,1024]{2,0,1:T(2,128)} %reshape.642), calls=%async_computation.3 | async-start | bytes 2097152 | tf_op jit(solution)/shard_map/all_to_all | solution.py:81
Sparse Core Ops, SparseCore 0:
  59.0 148.5 all-gather.1
where the time goes:
time: 327 us; the launch traced here: 325 us
  waiting for transfers between devices  168 us (51%)
  local copies, waits for them, and re-layouts  57.7 us (18%)
  blocking collectives  34.8 us (11%)
  other arithmetic  21.3 us (7%)
  starting transfers between devices  18.1 us (6%)
  between operations  13.8 us (4%)
  matrix products  11.4 us (3%)
    all_gather x1, waiting for transfers between devices, local(): everyone = lax.all_gather(query_local, 'serve', axis=1, tiled=True)  123 us
    unnamed x19, local copies, waits for them, and re-layouts  33 us
    all_to_all x1, waiting for transfers between devices, local(): lax.all_to_all(stacked_out, 'serve', split_axis=1, concat_axis=1, tiled=T...  32.3 us
    all_to_all x1, blocking collectives, local(): lax.all_to_all(attended, 'head', split_axis=1, concat_axis=2, tiled=True)  20.2 us
    all_to_all x1, blocking collectives, local(): lax.all_to_all(queries, 'head', split_axis=2, concat_axis=1, tiled=True)  14.5 us
    another operation x1, other arithmetic, local(): rank_table = jnp.cumsum(present.astype(jnp.int32), axis=2) - 1  14.4 us
    all_to_all x1, waiting for transfers between devices, local(): lax.all_to_all(stacked_log, 'serve', split_axis=1, concat_axis=1, tiled=T...  12.2 us
    all_to_all x1, local copies, waits for them, and re-layouts, local(): lax.all_to_all(queries, 'head', split_axis=2, concat_axis=1, tiled=True)  10.7 us
  transfers between devices with their start and end apart: 4, of which 3 were waited for; matrix products, arithmetic and copies ran while one was open for 15% of the time, Pallas kernels for 0%

commit v1 on v0

v1 whole, which is shorter than its diff:
```python
import functools

import jax
import jax.numpy as jnp
from jax import lax
from jax.experimental import pallas as pl
from jax.experimental.pallas import tpu as pltpu
from jax.sharding import PartitionSpec as P

NZ = 16
G = 8
MESH = pl.DeviceIdType.MESH
F32 = jnp.float32
BF16 = jnp.bfloat16
LOG2E = 1.4426950408889634


def dot(a, b, dims):
    return lax.dot_general(a, b, (dims, ((), ())), preferred_element_type=F32)


def wait_bytes(ref, sem):
    pltpu.make_async_copy(ref, ref, sem).wait()


def kernel(
    cfg,
    q_ref, fresh_ref, slot_ref, len_ref, owner_ref, suffix_ref, prefix_ref,
    out_ref,
    stage, hsend, hin, table_v, table_s, qsend, qin, osend, oin, lsend, lin,
    suffix, prefix, own_out, own_lse, asend, ain, scores,
    prefix_sem, suffix_sem, table_sem, hsend_sem, hrecv_sem, qsend_sem, qrecv_sem,
    osend_sem, orecv_sem, lsend_sem, lrecv_sem, asend_sem, arecv_sem,
):
    steps, per, heads, ny, nz, prompts, slab = cfg
    serve = ny * nz
    host = per * heads
    hd = 128
    rows = steps * G
    me_s = lax.axis_index("serve")
    me_h = lax.axis_index("head")
    my_y, my_z = me_s // nz, me_s % nz
    scale = hd**-0.5

    def ahead(shift):
        y, z = (my_y + shift // nz) % ny, (my_z + shift % nz) % nz
        return y * nz + z

    def behind(shift):
        y, z = (my_y - shift // nz + ny) % ny, (my_z - shift % nz + nz) % nz
        return y * nz + z

    barrier = pltpu.get_barrier_semaphore()

    def greet_serve(i, _):
        pl.semaphore_signal(barrier, inc=1, device_id=(ahead(i), me_h), device_id_type=MESH)
        return 0

    def greet_head(i, _):
        pl.semaphore_signal(
            barrier, inc=1, device_id=(me_s, (me_h + i) % heads), device_id_type=MESH
        )
        return 0

    if heads > 1:
        lax.fori_loop(1, heads, greet_head, 0)
    lax.fori_loop(1, serve, greet_serve, 0)

    prefix_copy = pltpu.make_async_copy(prefix_ref, prefix, prefix_sem)
    suffix_copy = pltpu.make_async_copy(suffix_ref, suffix, suffix_sem)
    prefix_copy.start()
    suffix_copy.start()

    lane = lax.broadcasted_iota(jnp.int32, (host, 128), 1)
    sub = lax.broadcasted_iota(jnp.int32, (host, 128), 0)
    wanted = sub + me_s * host
    found = jnp.zeros((host, 128), jnp.int32)
    for r in range(slot_ref.shape[0]):
        here = jnp.broadcast_to(slot_ref[r : r + 1, :], (host, 128)) == wanted
        held = (r * 128 + lane) // serve * 256 + jnp.broadcast_to(len_ref[r : r + 1, :], (host, 128))
        found = found + jnp.where(here, held, 0)
    found = jnp.broadcast_to(jnp.sum(found, axis=1, keepdims=True), (host, 128))
    prompt_of = found // 256
    length_of = found - prompt_of * 256
    halves = []
    for i in range(2):
        half = jnp.zeros((host, 128), jnp.int32)
        for p in range(prompts):
            half = jnp.where(prompt_of == p, owner_ref[p, i], half)
        halves.append(half)
    sent = jnp.where((halves[0] == lane) | (halves[1] == lane), sub, 0)
    table_v[0:host, :] = jnp.where(
        lane == 0, halves[0], jnp.where(lane == 1, halves[1], length_of)
    )
    table_v[host : host + 8, :] = jnp.broadcast_to(jnp.max(sent, axis=0, keepdims=True), (8, 128))
    table_copy = pltpu.make_async_copy(table_v, table_s, table_sem)
    table_copy.start()

    for t in range(steps):
        wide = q_ref[t].astype(F32)
        for c in range(heads):
            for g in range(G):
                col = (c * G + g) * hd
                stage[c, pl.ds(t * G + g, per, stride=rows), :] = wide[:, col : col + hd]
        wide = fresh_ref[t].astype(F32)
        for c in range(heads):
            for kv in range(2):
                base = per * rows + kv * rows
                col = (2 * c + kv) * hd
                stage[c, pl.ds(base + t, per, stride=steps), :] = wide[:, col : col + hd]
    used = per * steps
    for c in range(heads):
        for kv in range(2):
            base = per * rows + kv * rows
            stage[c, base + used : base + rows, :] = jnp.zeros((rows - used, hd), F32)
        hsend[c] = stage[c].astype(BF16).reshape(per + 2, rows, hd)

    pl.semaphore_wait(barrier, serve - 1 + heads - 1)

    def send_head(i, _):
        c = (me_h + i) % heads
        pltpu.make_async_remote_copy(
            src_ref=hsend.at[c],
            dst_ref=hin.at[me_h],
            send_sem=hsend_sem,
            recv_sem=hrecv_sem,
            device_id=(me_s, c),
            device_id_type=MESH,
        ).start()
        return 0

    if heads > 1:
        lax.fori_loop(1, heads, send_head, 0)
    hin[me_h] = hsend[me_h]
    table_copy.wait()
    if heads > 1:
        wait_bytes(hin.at[pl.ds(0, heads - 1)], hrecv_sem)

    def gather(shift, d):
        for j in range(2):
            k = table_s[host, d * 2 + j]
            qsend[shift, j] = hin[k // per, k % per]

    gather(0, me_s)
    qin[0] = qsend[0]

    def send_queries(shift, _):
        d = ahead(shift)
        gather(shift, d)
        pltpu.make_async_remote_copy(
            src_ref=qsend.at[shift],
            dst_ref=qin.at[shift],
            send_sem=qsend_sem,
            recv_sem=qrecv_sem.at[shift // nz],
            device_id=(d, me_h),
            device_id_type=MESH,
        ).start()
        return 0

    lax.fori_loop(1, serve, send_queries, 0)

    suffix_copy.wait()
    col = lax.broadcasted_iota(jnp.int32, (host * rows, heads * rows), 1)
    row = lax.broadcasted_iota(jnp.int32, (host * rows, heads * rows), 0)
    col_sample = col // rows * per + col % rows // steps
    live = (
        (col_sample == row // rows) & (col % rows < used) & (col % steps <= row % rows // G)
    )
    q_all = hin[:, 0:per].reshape(host * rows, hd)
    fresh_k = hin[:, per].reshape(heads * rows, hd)
    fresh_v = hin[:, per + 1].reshape(heads * rows, hd)
    fresh_scores = jnp.where(live, dot(q_all, fresh_k, ((1,), (1,))), -jnp.inf)
    lanes16 = lax.broadcasted_iota(jnp.int32, (rows, 128), 1)

    def own_scores(k, _):
        s = dot(hin[k // per, k % per], suffix[k, 0], ((1,), (1,)))
        scores[k] = jnp.where(lanes16 < table_s[k, 2], s, -jnp.inf)
        return 0

    lax.fori_loop(0, host, own_scores, 0)
    cache_scores = scores[...].reshape(host * rows, 128)
    top = jnp.maximum(
        jnp.max(cache_scores, axis=1, keepdims=True), jnp.max(fresh_scores, axis=1, keepdims=True)
    )
    cache_exp = jnp.exp((cache_scores - top) * scale)
    fresh_exp = jnp.exp((fresh_scores - top) * scale)
    total = jnp.sum(cache_exp, axis=1, keepdims=True) + jnp.sum(fresh_exp, axis=1, keepdims=True)
    scores[...] = cache_exp.reshape(host, rows, 128)
    own_out[...] = dot(fresh_exp.astype(BF16), fresh_v, ((1,), (0,))).reshape(host, rows, hd)
    own_lse[...] = jnp.broadcast_to(top * scale + jnp.log(total), (host * rows, 128)).reshape(
        host, rows, 128
    )
    inverse = jnp.broadcast_to(1.0 / total, (host * rows, 128)).reshape(host, rows, 128)

    def own_values(k, _):
        own_out[k] = own_out[k] + dot(scores[k].astype(BF16), suffix[k, 1], ((1,), (0,)))
        return 0

    lax.fori_loop(0, host, own_values, 0)
    own_out[...] = own_out[...] * inverse

    prefix_copy.wait()
    tile = nz * rows

    def group(r, _):
        @pl.when(r == 0)
        def _():
            wait_bytes(qin.at[pl.ds(1, nz - 1)], qrecv_sem.at[0])

        @pl.when(r > 0)
        def _():
            wait_bytes(qin.at[pl.ds(0, nz)], qrecv_sem.at[r])

        first = r * nz

        def half(j, _):
            q = qin[pl.ds(first, nz), j].reshape(tile, hd)
            s = dot(q, prefix[j, 0], ((1,), (1,)))
            top = jnp.max(s, axis=1, keepdims=True)
            p = jnp.exp2(s * (scale * LOG2E) - top * (scale * LOG2E))
            total = jnp.sum(p, axis=1, keepdims=True)
            o = dot(p.astype(BF16), prefix[j, 1], ((1,), (0,))) / total
            osend[pl.ds(first, nz), j] = o.astype(BF16).reshape(nz, rows, hd)
            lse = jnp.broadcast_to(top * scale + jnp.log(total), (tile, 128))
            for b in range(tile // 128):
                flat = jnp.transpose(lse[b * 128 : (b + 1) * 128, :])
                lsend[r * (tile // 128) + b, pl.ds(j, 1), :] = flat[0:1, :]
            return 0

        lax.fori_loop(0, 2, half, 0)

        def send_back(shift, _):
            @pl.when(shift > 0)
            def _():
                d = behind(shift)
                pltpu.make_async_remote_copy(
                    src_ref=osend.at[shift],
                    dst_ref=oin.at[shift],
                    send_sem=osend_sem,
                    recv_sem=orecv_sem,
                    device_id=(d, me_h),
                    device_id_type=MESH,
                ).start()
                pltpu.make_async_remote_copy(
                    src_ref=lsend.at[shift // 8],
                    dst_ref=lin.at[shift],
                    send_sem=lsend_sem,
                    recv_sem=lrecv_sem,
                    device_id=(d, me_h),
                    device_id_type=MESH,
                ).start()

            return 0

        lax.fori_loop(first, first + nz, send_back, 0)
        return 0

    lax.fori_loop(0, ny, group, 0)
    oin[0] = osend[0]
    lin[0] = lsend[0]
    wait_bytes(lin.at[pl.ds(1, serve - 1)], lrecv_sem)
    wait_bytes(oin.at[pl.ds(1, serve - 1)], orecv_sem)

    sub16 = lax.broadcasted_iota(jnp.int32, (rows, 128), 0)

    def combine(k, _):
        outs, logs = [], []
        for i in range(2):
            h = table_s[k, i]
            d, j = h // 2, h % 2
            z = (d % nz - my_z + nz) % nz
            shift = (d // nz - my_y + ny) % ny * nz + z
            outs.append(oin[shift, j].astype(F32))
            line = jnp.broadcast_to(lin[shift, pl.ds(j, 1), :], (rows, 128))
            mine = lanes16 == sub16 + z % 8 * rows
            logs.append(jnp.sum(jnp.where(mine, line, 0.0), axis=1, keepdims=True))
        own = own_lse[k]
        top = jnp.maximum(jnp.maximum(logs[0], logs[1]), own)
        a0, a1, a2 = jnp.exp(logs[0] - top), jnp.exp(logs[1] - top), jnp.exp(own - top)
        mixed = (a0 * outs[0] + a1 * outs[1] + a2 * own_out[k]) / (a0 + a1 + a2)
        asend[k // per, k % per] = mixed.astype(BF16)
        return 0

    lax.fori_loop(0, host, combine, 0)

    def send_out(i, _):
        c = (me_h + i) % heads
        pltpu.make_async_remote_copy(
            src_ref=asend.at[c],
            dst_ref=ain.at[me_h],
            send_sem=asend_sem,
            recv_sem=arecv_sem,
            device_id=(me_s, c),
            device_id_type=MESH,
        ).start()
        return 0

    if heads > 1:
        lax.fori_loop(1, heads, send_out, 0)
    ain[me_h] = asend[me_h]
    if heads > 1:
        wait_bytes(ain.at[pl.ds(0, heads - 1)], arecv_sem)
    for c in range(heads):
        stage[c, 0 : per * rows, :] = ain[c].astype(F32).reshape(per * rows, hd)
    for t in range(steps):
        for c in range(heads):
            for g in range(G):
                col = (c * G + g) * hd
                out_ref[t, :, col : col + hd] = stage[
                    c, pl.ds(t * G + g, per, stride=rows), :
                ].astype(BF16)

    wait_bytes(qsend.at[pl.ds(0, serve - 1)], qsend_sem)
    wait_bytes(osend.at[pl.ds(0, serve - 1)], osend_sem)
    wait_bytes(lin.at[pl.ds(0, serve - 1)], lsend_sem)
    if heads > 1:
        wait_bytes(hsend.at[pl.ds(0, heads - 1)], hsend_sem)
        wait_bytes(asend.at[pl.ds(0, heads - 1)], asend_sem)


def local(queries, new_kv, suffix_kv, prefix_kv, owner_map, host_slot, suffix_len):
    serve, heads = lax.axis_size("serve"), lax.axis_size("head")
    steps, per = queries.shape[0], queries.shape[1]
    host, slab = suffix_kv.shape[0], prefix_kv.shape[3]
    nz = NZ
    ny = serve // nz
    rows, hd = steps * G, 128
    cfg = (steps, per, heads, ny, nz, owner_map.shape[0], slab)
    dma = pltpu.SemaphoreType.DMA
    vmem = pl.BlockSpec(memory_space=pltpu.VMEM)
    smem = pl.BlockSpec(memory_space=pltpu.SMEM)
    hbm = pl.BlockSpec(memory_space=pltpu.HBM)
    return pl.pallas_call(
        functools.partial(kernel, cfg),
        out_shape=jax.ShapeDtypeStruct(queries.shape, BF16),
        in_specs=[vmem, vmem, vmem, vmem, smem, hbm, hbm],
        out_specs=vmem,
        scratch_shapes=[
            pltpu.VMEM((heads, (per + 2) * rows, hd), F32),
            pltpu.VMEM((heads, per + 2, rows, hd), BF16),
            pltpu.VMEM((heads, per + 2, rows, hd), BF16),
            pltpu.VMEM((host + 8, 128), jnp.int32),
            pltpu.SMEM((host + 8, 128), jnp.int32),
            pltpu.VMEM((serve, 2, rows, hd), BF16),
            pltpu.VMEM((serve, 2, rows, hd), BF16),
            pltpu.VMEM((serve, 2, rows, hd), BF16),
            pltpu.VMEM((serve, 2, rows, hd), BF16),
            pltpu.VMEM((serve // 8, 2, 128), F32),
            pltpu.VMEM((serve, 2, 128), F32),
            pltpu.VMEM((host, 2, 128, hd), BF16),
            pltpu.VMEM((2, 2, slab, hd), BF16),
            pltpu.VMEM((host, rows, hd), F32),
            pltpu.VMEM((host, rows, 128), F32),
            pltpu.VMEM((heads, per, rows, hd), BF16),
            pltpu.VMEM((heads, per, rows, hd), BF16),
            pltpu.VMEM((host, rows, 128), F32),
            dma, dma, dma, dma, dma, dma, dma((ny,)), dma, dma, dma, dma, dma, dma,
        ],
        compiler_params=pltpu.CompilerParams(
            collective_id=0, has_side_effects=True, vmem_limit_bytes=56 * 1024 * 1024
        ),
    )(
        queries,
        new_kv,
        host_slot.reshape(-1, 128),
        suffix_len.reshape(-1, 128),
        owner_map,
        suffix_kv.reshape(host, 2, 128, hd),
        prefix_kv.reshape(2, 2, slab, hd),
    )


def solution(mesh):
    return jax.shard_map(
        local,
        mesh=mesh,
        in_specs=(
            P(None, ("serve", "head"), None),
            P(None, ("serve", "head"), None),
            P("serve", "head", None, None, None),
            P("serve", "head", None, None, None),
            P(),
            P(),
            P(),
        ),
        out_specs=P(None, ("serve", "head"), None),
        check_vma=False,
    )
```

time: 327 us -> 89.5 us (0.27)
  waiting for transfers between devices: 168 us -> 0 us
  Pallas kernels: 0 us -> 86.3 us
  local copies, waits for them, and re-layouts: 57.7 us -> 2.97 us
  blocking collectives: 34.8 us -> 0 us
  other arithmetic: 21.3 us -> 0 us
  starting transfers between devices: 18.1 us -> 0 us
  between operations: 13.8 us -> 0.01 us
  matrix products: 11.4 us -> 0 us
    all_gather x1 -> x0, waiting for transfers between devices: 123 us -> none  [local(): everyone = lax.all_gather(query_local, 'serve', axis=1, tiled=True)]
    pallas_call x0 -> x1, Pallas kernels: none -> 86.3 us  [local(): pl.pallas_call(functools.partial(kernel, cfg), out_shape=jax.ShapeDtypeSt...]
    all_to_all x3 -> x0, waiting for transfers between devices: 44.6 us -> none  [the longest x1 32.3 us: local(): lax.all_to_all(stacked_out, 'serve', split_axis=1, concat_axis=1, tiled=T...]
    all_to_all x2 -> x0, blocking collectives: 34.8 us -> none  [the longest x1 20.2 us: local(): lax.all_to_all(attended, 'head', split_axis=1, concat_axis=2, tiled=True)]
    unnamed x19 -> x2, local copies, waits for them, and re-layouts: 33 us -> 2.97 us
    all_to_all x3 -> x0, starting transfers between devices: 18.1 us -> none  [the longest x1 8.83 us: local(): lax.all_to_all(stacked_log, 'serve', split_axis=1, concat_axis=1, tiled=T...]
    another operation x3 -> x0, other arithmetic: 14.5 us -> none  [the longest x1 14.4 us: local(): rank_table = jnp.cumsum(present.astype(jnp.int32), axis=2) - 1]
    all_to_all x4 -> x0, local copies, waits for them, and re-layouts: 12.2 us -> none  [the longest x1 10.7 us: local(): lax.all_to_all(queries, 'head', split_axis=2, concat_axis=1, tiled=True)]
  transfers between devices with their start and end apart: 4 -> 0, of which waited for: 3 -> 0; matrix products, arithmetic and copies ran while one was open for 15% -> 0% of each run, Pallas kernels for 0% -> 0%
where the time goes in v1:
time: 89.5 us; the launch traced here: 89.3 us
  Pallas kernels  86.3 us (96%)
  local copies, waits for them, and re-layouts  2.97 us (3%)
    pallas_call x1, Pallas kernels, local(): pl.pallas_call(functools.partial(kernel, cfg), out_shape=jax.ShapeDtypeSt...  86.3 us
    unnamed x2, local copies, waits for them, and re-layouts  2.97 us

profile of v1, /device:TPU:1, one launch (start us, length us, event | category | flops | bytes accessed | tf_op | source)
XLA Modules:
  0.0 89.3 jit_solution(16956166015116869595)
XLA Ops:
  0.0 1.4 %copy.8.owner_ref = s32[32,2]{1,0:T(8,128)} copy(s32[32,2]{0,1:T(2,128)} %param.11) | data formatting | bytes 512 | tf_op args[4]
  1.4 86.3 %shard_map.73 = bf16[2,4,8192]{2,1,0:T(4,128)(2,1)} custom-call(bf16[2,4,8192]{2,1,0:T(4,128)(2,1)} %q_ref.1, bf16[2,4,2048]{2,1,0:T(4,128)(2,1)} %fresh_ref.1, s32[16,128]{1,0:T(8,128)} %bitcast.6, s32[16,128]{1,0:T(8,128)} %bitcast.7, s32[32,2]{1,0:T(8,128)} %copy.8.owner_ref, bf16[32,2,128,128]{3,2,1,0:T(8,128)(2,1)} %bitcast.4, ...), custom_call_target="tpu_custom_call" | custom-call | tf_op jit(solution)/shard_map/pallas_call | solution.py:333
  87.7 1.6 %copy.10 = bf16[2,4,8192]{2,1,0:T(4,128)(2,1)} copy(bf16[2,4,8192]{2,1,0:T(4,128)(2,1)} %shard_map.73) | data formatting | bytes 262144

commit v2 on v1

v2 whole, which is shorter than its diff:
```python
import functools

import jax
import jax.numpy as jnp
from jax import lax
from jax.experimental import pallas as pl
from jax.experimental.pallas import tpu as pltpu
from jax.sharding import PartitionSpec as P

NZ = 16
G = 8
MESH = pl.DeviceIdType.MESH
F32 = jnp.float32
BF16 = jnp.bfloat16
LOG2E = 1.4426950408889634


def dot(a, b, dims):
    return lax.dot_general(a, b, (dims, ((), ())), preferred_element_type=F32)


def wait_bytes(ref, sem):
    pltpu.make_async_copy(ref, ref, sem).wait()


def kernel(
    cfg,
    q_hbm, fresh_hbm, slot_hbm, len_hbm, owner_hbm, suffix_hbm, prefix_hbm,
    out_ref,
    q_ref, fresh_ref, slot_ref, len_ref, owner_ref, suffix, prefix,
    stage, hsend, hin, fsend, fin, table_v, table_s,
    qsend, qin, osend, oin, lflat, lsend, lin,
    own_out, own_lse, scores, asend, ain,
    load_sem, table_sem, head_sem, fresh_sem, out_sem,
    qrecv_sem, qsend_sem, osend_sem, lse_sem,
):
    steps, per, heads, ny, nz, prompts = cfg
    serve = ny * nz
    host = per * heads
    hd = 128
    rows = steps * G
    far = nz // 2
    me_s = lax.axis_index("serve")
    me_h = lax.axis_index("head")
    my_y, my_z = me_s // nz, me_s % nz
    scale = hd**-0.5

    def at(y, z):
        return ((my_y + y) & (ny - 1)) * nz + ((my_z + z) & (nz - 1))

    mine = serve - ny

    def distance(n):
        i = n // ny
        if isinstance(n, int):
            return n % ny, far - (i + 1) // 2 if i % 2 == 1 else far + i // 2
        return n % ny, jnp.where(i % 2 == 1, far - (i + 1) // 2, far + i // 2)

    def ahead(n):
        return at(*distance(n))

    def behind(n):
        y, z = distance(n)
        return at(-y, -z)

    def send(src, dst, send_sem, recv_sem, s, h):
        pltpu.make_async_remote_copy(
            src_ref=src,
            dst_ref=dst,
            send_sem=send_sem,
            recv_sem=recv_sem,
            device_id=(s, h),
            device_id_type=MESH,
        ).start()

    def fori(low, high, body):
        def step(i, _):
            body(i)
            return 0

        lax.fori_loop(low, high, step, 0)

    loads = [
        pltpu.make_async_copy(src, dst, load_sem.at[i])
        for i, (src, dst) in enumerate(
            (
                (q_hbm, q_ref),
                (fresh_hbm, fresh_ref),
                (slot_hbm, slot_ref),
                (len_hbm, len_ref),
                (owner_hbm, owner_ref),
                (prefix_hbm, prefix),
                (suffix_hbm, suffix),
            )
        )
    ]
    for load in loads:
        load.start()

    barrier = pltpu.get_barrier_semaphore()

    def greet(s, h):
        pl.semaphore_signal(barrier, inc=1, device_id=(s, h), device_id_type=MESH)

    for n in range(serve):
        if n != mine:
            greet(ahead(n), me_h)
    for i in range(1, heads):
        greet(me_s, (me_h + i) & (heads - 1))

    loads[0].wait()
    for t in range(steps):
        wide = q_ref[t].astype(F32)
        for c in range(heads):
            for g in range(G):
                col = (c * G + g) * hd
                stage[c, pl.ds(t * G + g, per, stride=rows), :] = wide[:, col : col + hd]
    for c in range(heads):
        hsend[c] = stage[c].astype(BF16).reshape(per, rows, hd)
    used = per * steps
    loads[1].wait()
    for t in range(steps):
        wide = fresh_ref[t].astype(F32)
        for c in range(heads):
            for kv in range(2):
                col = (2 * c + kv) * hd
                stage[c, pl.ds(kv * rows + t, per, stride=steps), :] = wide[:, col : col + hd]
    for c in range(heads):
        for kv in range(2):
            stage[c, kv * rows + used : (kv + 1) * rows, :] = jnp.zeros((rows - used, hd), F32)
        fsend[c] = stage[c, 0 : 2 * rows, :].astype(BF16).reshape(2, rows, hd)

    for i in (2, 3, 4):
        loads[i].wait()
    lane = lax.broadcasted_iota(jnp.int32, (host, 128), 1)
    sub = lax.broadcasted_iota(jnp.int32, (host, 128), 0)
    wanted = sub + me_s * host
    found = jnp.zeros((host, 128), jnp.int32)
    for r in range(slot_ref.shape[0]):
        here = jnp.broadcast_to(slot_ref[r : r + 1, :], (host, 128)) == wanted
        held = (r * 128 + lane) // serve * 256 + jnp.broadcast_to(len_ref[r : r + 1, :], (host, 128))
        found = found + jnp.where(here, held, 0)
    found = jnp.broadcast_to(jnp.sum(found, axis=1, keepdims=True), (host, 128))
    prompt_of = found >> 8
    places, sent = [], sub * 0
    for i in range(2):
        half = sub * 0
        for p in range(prompts):
            half = jnp.where(prompt_of == p, owner_ref[i, p], half)
        sent = jnp.where(half == lane, sub, sent)
        y = ((half >> 1) // nz - my_y) & (ny - 1)
        z = ((half >> 1) - my_z) & (nz - 1)
        i = jnp.where(z < far, 2 * (far - z) - 1, 2 * (z - far))
        places.append((i * ny + y) * 2 + (half & 1))
    table_v[0:host, :] = jnp.where(
        lane == 0, places[0], jnp.where(lane == 1, places[1], found & 255)
    )
    table_v[host : host + 8, :] = jnp.broadcast_to(jnp.max(sent, axis=0, keepdims=True), (8, 128))
    table_copy = pltpu.make_async_copy(table_v, table_s, table_sem)
    table_copy.start()

    pl.semaphore_wait(barrier, serve - 1 + heads - 1)

    def send_head(i):
        c = (me_h + i) & (heads - 1)
        send(hsend.at[c], hin.at[me_h], head_sem.at[0], head_sem.at[1], me_s, c)

    def send_fresh(i):
        c = (me_h + i) & (heads - 1)
        send(fsend.at[c], fin.at[me_h], fresh_sem.at[0], fresh_sem.at[1], me_s, c)

    fori(1, heads, send_head)
    fori(1, heads, send_fresh)
    hin[me_h] = hsend[me_h]
    fin[me_h] = fsend[me_h]
    table_copy.wait()
    wait_bytes(hin.at[pl.ds(0, heads - 1)], head_sem.at[1])

    def pick(d, j):
        k = table_s[host, d * 2 + j]
        return hin[k // per, k % per]

    def gather(shift, d):
        for j in range(2):
            qsend[shift, j] = pick(d, j)

    def send_queries(n):
        d = ahead(n)
        gather(n, d)
        send(qsend.at[n], qin.at[n], qsend_sem, qrecv_sem.at[n // nz], d, me_h)

    fori(0, mine, send_queries)
    fori(mine + 1, serve, send_queries)
    gather(mine, me_s)
    qin[mine] = qsend[mine]

    loads[6].wait()
    lanes16 = lax.broadcasted_iota(jnp.int32, (rows, 128), 1)
    sub16 = lax.broadcasted_iota(jnp.int32, (rows, 128), 0)

    def own_scores(c):
        for i in range(per):
            k = c * per + i
            s = dot(hin[c, i], suffix[k, 0], ((1,), (1,)))
            scores[k] = jnp.where(lanes16 < table_s[k, 2], s, -jnp.inf)

    fori(0, heads, own_scores)
    wait_bytes(fin.at[pl.ds(0, heads - 1)], fresh_sem.at[1])
    col = lax.broadcasted_iota(jnp.int32, (host * rows, heads * rows), 1)
    row = lax.broadcasted_iota(jnp.int32, (host * rows, heads * rows), 0)
    col_sample = col // rows * per + col % rows // steps
    live = (
        (col_sample == row // rows) & (col % rows < used) & (col % steps <= row % rows // G)
    )
    q_all = hin[...].reshape(host * rows, hd)
    fresh_k = fin[:, 0].reshape(heads * rows, hd)
    fresh_v = fin[:, 1].reshape(heads * rows, hd)
    fresh_scores = jnp.where(live, dot(q_all, fresh_k, ((1,), (1,))), -jnp.inf)
    cache_scores = scores[...].reshape(host * rows, 128)
    top = jnp.maximum(
        jnp.max(cache_scores, axis=1, keepdims=True), jnp.max(fresh_scores, axis=1, keepdims=True)
    )
    cache_exp = jnp.exp((cache_scores - top) * scale)
    fresh_exp = jnp.exp((fresh_scores - top) * scale)
    total = jnp.sum(cache_exp, axis=1, keepdims=True) + jnp.sum(fresh_exp, axis=1, keepdims=True)
    scores[...] = cache_exp.reshape(host, rows, 128)
    own_out[...] = dot(fresh_exp.astype(BF16), fresh_v, ((1,), (0,))).reshape(host, rows, hd)
    own_lse[...] = jnp.broadcast_to(top * scale + jnp.log(total), (host * rows, 128)).reshape(
        host, rows, 128
    )
    inverse = jnp.broadcast_to(1.0 / total, (host * rows, 128)).reshape(host, rows, 128)

    def own_values(c):
        for i in range(per):
            k = c * per + i
            own_out[k] = own_out[k] + dot(scores[k].astype(BF16), suffix[k, 1], ((1,), (0,)))

    fori(0, heads, own_values)
    own_out[...] = own_out[...] * inverse

    loads[5].wait()
    tile = nz * rows

    def group(r):
        @pl.when(r == ny - 1)
        def _():
            wait_bytes(qin.at[pl.ds(0, nz - 1)], qrecv_sem.at[ny - 1])

        @pl.when(r < ny - 1)
        def _():
            wait_bytes(qin.at[pl.ds(0, nz)], qrecv_sem.at[r])

        first = r * nz

        def half(j):
            q = qin[pl.ds(first, nz), j].reshape(tile, hd)
            s = dot(q, prefix[j, 0], ((1,), (1,)))
            top = jnp.max(s, axis=1, keepdims=True)
            p = jnp.exp2(s * (scale * LOG2E) - top * (scale * LOG2E))
            total = jnp.sum(p, axis=1, keepdims=True)
            o = dot(p.astype(BF16), prefix[j, 1], ((1,), (0,))) / total
            osend[pl.ds(first, nz), j] = o.astype(BF16).reshape(nz, rows, hd)
            lse = jnp.broadcast_to(top * scale + jnp.log(total), (tile, 128))
            for b in range(tile // 128):
                lflat[j, b : b + 1, :] = jnp.transpose(lse[b * 128 : (b + 1) * 128, :])[0:1, :]

        fori(0, 2, half)
        low = lax.broadcasted_iota(jnp.int32, (1, 128), 1) < 64
        for b in range(tile // 128):
            line0, line1 = lflat[0, b : b + 1, :], lflat[1, b : b + 1, :]
            place = r * (nz // 4) + b * 2
            lsend[place] = jnp.where(low, line0, pltpu.roll(line1, 64, 1))
            lsend[place + 1] = jnp.where(low, pltpu.roll(line0, 64, 1), line1)

        def send_lse(n):
            send(lsend.at[n // 4], lin.at[n], lse_sem.at[0], lse_sem.at[1], behind(n), me_h)

        def send_back(n):
            send(osend.at[n], oin.at[n], osend_sem.at[0], osend_sem.at[1], behind(n), me_h)

        stop = jnp.where(r == ny - 1, mine, first + nz)
        fori(first, stop, send_lse)
        fori(first, stop, send_back)

        @pl.when(r == ny - 1)
        def _():
            fori(mine + 1, serve, send_lse)
            fori(mine + 1, serve, send_back)

    fori(0, ny, group)
    oin[mine] = osend[mine]
    lin[mine] = lsend[mine // 4]
    wait_bytes(lin.at[pl.ds(0, serve - 1)], lse_sem.at[1])

    def weigh(c):
        for m in range(per):
            k = c * per + m
            logs = []
            for i in range(2):
                place = table_s[k, i]
                n = place >> 1
                line = jnp.broadcast_to(lin[n], (rows, 128))
                here = lanes16 == sub16 + (n & 3) * rows + (place & 1) * 64
                logs.append(jnp.sum(jnp.where(here, line, 0.0), axis=1, keepdims=True))
            own = own_lse[k]
            top = jnp.maximum(jnp.maximum(logs[0], logs[1]), own)
            a0, a1, a2 = jnp.exp(logs[0] - top), jnp.exp(logs[1] - top), jnp.exp(own - top)
            inverse = 1.0 / (a0 + a1 + a2)
            scores[k] = a0 * inverse
            own_lse[k] = a1 * inverse
            own_out[k] = own_out[k] * (a2 * inverse)

    fori(0, heads, weigh)
    wait_bytes(oin.at[pl.ds(0, serve - 1)], osend_sem.at[1])

    def mix(c, dst):
        for n in range(per):
            k = c * per + n
            p0, p1 = table_s[k, 0], table_s[k, 1]
            half0 = oin[p0 >> 1, p0 & 1].astype(F32)
            half1 = oin[p1 >> 1, p1 & 1].astype(F32)
            dst[c, n] = (scores[k] * half0 + own_lse[k] * half1 + own_out[k]).astype(BF16)

    def send_out(i):
        c = (me_h + i) & (heads - 1)
        mix(c, asend)
        send(asend.at[c], ain.at[me_h], out_sem.at[0], out_sem.at[1], me_s, c)

    fori(1, heads, send_out)
    mix(me_h, ain)
    wait_bytes(ain.at[pl.ds(0, heads - 1)], out_sem.at[1])
    for c in range(heads):
        stage[c] = ain[c].astype(F32).reshape(per * rows, hd)
    for t in range(steps):
        for c in range(heads):
            for g in range(G):
                col = (c * G + g) * hd
                out_ref[t, :, col : col + hd] = stage[
                    c, pl.ds(t * G + g, per, stride=rows), :
                ].astype(BF16)

    wait_bytes(qsend.at[pl.ds(0, serve - 1)], qsend_sem)
    wait_bytes(osend.at[pl.ds(0, serve - 1)], osend_sem.at[0])
    wait_bytes(lin.at[pl.ds(0, serve - 1)], lse_sem.at[0])
    wait_bytes(hsend.at[pl.ds(0, heads - 1)], head_sem.at[0])
    wait_bytes(fsend.at[pl.ds(0, heads - 1)], fresh_sem.at[0])
    wait_bytes(asend.at[pl.ds(0, heads - 1)], out_sem.at[0])


def local(queries, new_kv, suffix_kv, prefix_kv, owner_map, host_slot, suffix_len):
    serve, heads = lax.axis_size("serve"), lax.axis_size("head")
    steps, per = queries.shape[0], queries.shape[1]
    host, slab = suffix_kv.shape[0], prefix_kv.shape[3]
    prompts, samples = owner_map.shape[0], host_slot.shape[0]
    nz = NZ
    ny = serve // nz
    rows, hd = steps * G, 128
    cfg = (steps, per, heads, ny, nz, prompts)
    dma = pltpu.SemaphoreType.DMA
    hbm = pl.BlockSpec(memory_space=pltpu.HBM)
    return pl.pallas_call(
        functools.partial(kernel, cfg),
        out_shape=pltpu.VMEM(queries.shape, BF16),
        in_specs=[hbm] * 7,
        out_specs=pl.BlockSpec(memory_space=pltpu.VMEM),
        scratch_shapes=[
            pltpu.VMEM(queries.shape, BF16),
            pltpu.VMEM(new_kv.shape, BF16),
            pltpu.VMEM((samples // 128, 128), jnp.int32),
            pltpu.VMEM((samples // 128, 128), jnp.int32),
            pltpu.SMEM((2, prompts), jnp.int32),
            pltpu.VMEM((host, 2, 128, hd), BF16),
            pltpu.VMEM((2, 2, slab, hd), BF16),
            pltpu.VMEM((heads, per * rows, hd), F32),
            pltpu.VMEM((heads, per, rows, hd), BF16),
            pltpu.VMEM((heads, per, rows, hd), BF16),
            pltpu.VMEM((heads, 2, rows, hd), BF16),
            pltpu.VMEM((heads, 2, rows, hd), BF16),
            pltpu.VMEM((host + 8, 128), jnp.int32),
            pltpu.SMEM((host + 8, 128), jnp.int32),
            pltpu.VMEM((serve, 2, rows, hd), BF16),
            pltpu.VMEM((serve, 2, rows, hd), BF16),
            pltpu.VMEM((serve, 2, rows, hd), BF16),
            pltpu.VMEM((serve, 2, rows, hd), BF16),
            pltpu.VMEM((2, 8, 128), F32),
            pltpu.VMEM((serve // 4, 1, 128), F32),
            pltpu.VMEM((serve, 1, 128), F32),
            pltpu.VMEM((host, rows, hd), F32),
            pltpu.VMEM((host, rows, 128), F32),
            pltpu.VMEM((host, rows, 128), F32),
            pltpu.VMEM((heads, per, rows, hd), BF16),
            pltpu.VMEM((heads, per, rows, hd), BF16),
            dma((7,)),
            dma,
            dma((2,)),
            dma((2,)),
            dma((2,)),
            dma((ny,)),
            dma,
            dma((2,)),
            dma((2,)),
        ],
        compiler_params=pltpu.CompilerParams(
            collective_id=0, has_side_effects=True, vmem_limit_bytes=57 * 1024 * 1024
        ),
    )(
        queries,
        new_kv,
        host_slot.reshape(-1, 128),
        suffix_len.reshape(-1, 128),
        owner_map.T,
        suffix_kv.reshape(host, 2, 128, hd),
        prefix_kv.reshape(2, 2, slab, hd),
    )


def solution(mesh):
    return jax.shard_map(
        local,
        mesh=mesh,
        in_specs=(
            P(None, ("serve", "head"), None),
            P(None, ("serve", "head"), None),
            P("serve", "head", None, None, None),
            P("serve", "head", None, None, None),
            P(),
            P(),
            P(),
        ),
        out_specs=P(None, ("serve", "head"), None),
        check_vma=False,
    )
```

time: 89.5 us -> 77.2 us (0.86)
  Pallas kernels: 86.3 us -> 76.4 us
  local copies, waits for them, and re-layouts: 2.97 us -> 0.66 us
    pallas_call x1, Pallas kernels: 86.3 us -> 76.4 us  [local(): pl.pallas_call(functools.partial(kernel, cfg), out_shape=pltpu.VMEM(queri...]
    unnamed x2 -> x1, local copies, waits for them, and re-layouts: 2.97 us -> 0.66 us
where the time goes in v2:
time: 77.2 us; the launch traced here: 77.1 us
  Pallas kernels  76.4 us (99%)
    pallas_call x1, Pallas kernels, local(): pl.pallas_call(functools.partial(kernel, cfg), out_shape=pltpu.VMEM(queri...  76.4 us

profile of v2, /device:TPU:1, one launch (start us, length us, event | category | flops | bytes accessed | tf_op | source)
XLA Modules:
  0.0 77.1 jit_solution(12544861919815569735)
XLA Ops:
  0.0 76.4 %shard_map.73 = bf16[2,4,8192]{2,1,0:T(4,128)(2,1)S(1)} custom-call(bf16[2,4,8192]{2,1,0:T(4,128)(2,1)} %q_hbm.1, bf16[2,4,2048]{2,1,0:T(4,128)(2,1)} %fresh_hbm.1, s32[16,128]{1,0:T(8,128)} %bitcast.7, s32[16,128]{1,0:T(8,128)} %bitcast.8, s32[2,32]{1,0:T(2,128)} %bitcast.9, bf16[32,2,128,128]{3,2,1,0:T(8,128)(2,1)} %bitcast.5, ...), custom_call_target="tpu_custom_call" | custom-call | tf_op jit(solution)/shard_map/pallas_call | solution.py:361
  76.4 0.7 copy.9

commit v3 on v2

--- a/solution.py
+++ b/solution.py
@@ -48,13 +48,13 @@
     def at(y, z):
         return ((my_y + y) & (ny - 1)) * nz + ((my_z + z) & (nz - 1))
 
-    mine = serve - ny
+    mine = nz - 1
 
     def distance(n):
-        i = n // ny
+        i = n % nz
         if isinstance(n, int):
-            return n % ny, far - (i + 1) // 2 if i % 2 == 1 else far + i // 2
-        return n % ny, jnp.where(i % 2 == 1, far - (i + 1) // 2, far + i // 2)
+            return n // nz, far - (i + 1) // 2 if i % 2 == 1 else far + i // 2
+        return n // nz, jnp.where(i % 2 == 1, far - (i + 1) // 2, far + i // 2)
 
     def ahead(n):
         return at(*distance(n))
@@ -151,7 +151,7 @@
         y = ((half >> 1) // nz - my_y) & (ny - 1)
         z = ((half >> 1) - my_z) & (nz - 1)
         i = jnp.where(z < far, 2 * (far - z) - 1, 2 * (z - far))
-        places.append((i * ny + y) * 2 + (half & 1))
+        places.append((y * nz + i) * 2 + (half & 1))
     table_v[0:host, :] = jnp.where(
         lane == 0, places[0], jnp.where(lane == 1, places[1], found & 255)
     )
@@ -242,11 +242,11 @@
     tile = nz * rows
 
     def group(r):
-        @pl.when(r == ny - 1)
+        @pl.when(r == 0)
         def _():
-            wait_bytes(qin.at[pl.ds(0, nz - 1)], qrecv_sem.at[ny - 1])
-
-        @pl.when(r < ny - 1)
+            wait_bytes(qin.at[pl.ds(0, nz - 1)], qrecv_sem.at[0])
+
+        @pl.when(r > 0)
         def _():
             wait_bytes(qin.at[pl.ds(0, nz)], qrecv_sem.at[r])
 
@@ -278,14 +278,33 @@
         def send_back(n):
             send(osend.at[n], oin.at[n], osend_sem.at[0], osend_sem.at[1], behind(n), me_h)
 
-        stop = jnp.where(r == ny - 1, mine, first + nz)
-        fori(first, stop, send_lse)
-        fori(first, stop, send_back)
+        def lse_other(n):
+            @pl.when(n != mine)
+            def _():
+                send_lse(n)
+
+        def send_some(q, k):
+            def one(n):
+                z = (my_z - distance(n)[1]) & (nz - 1)
+                quarter = jnp.minimum(z // (nz // 4), 2)
+
+                @pl.when((quarter == k) & (n != mine))
+                def _():
+                    send_back(n)
+
+            fori(q * nz, q * nz + nz, one)
+
+        fori(first, first + nz, lse_other)
+        for k in range(3):
+
+            @pl.when(r >= k)
+            def _(k=k):
+                send_some(r - k, k)
 
         @pl.when(r == ny - 1)
         def _():
-            fori(mine + 1, serve, send_lse)
-            fori(mine + 1, serve, send_back)
+            for k in range(3):
+                fori(ny - k, ny, lambda q, k=k: send_some(q, k))
 
     fori(0, ny, group)
     oin[mine] = osend[mine]

time: 77.2 us -> 74.8 us (0.969)
  Pallas kernels: 76.4 us -> 74.1 us
    pallas_call x1, Pallas kernels: 76.4 us -> 74.1 us  [local(): pl.pallas_call(functools.partial(kernel, cfg), out_shape=pltpu.VMEM(queri...]
where the time goes in v3:
time: 74.8 us; the launch traced here: 74.7 us
  Pallas kernels  74.1 us (99%)
    pallas_call x1, Pallas kernels, local(): pl.pallas_call(functools.partial(kernel, cfg), out_shape=pltpu.VMEM(queri...  74.1 us

profile of v3, /device:TPU:1, one launch (start us, length us, event | category | flops | bytes accessed | tf_op | source)
XLA Modules:
  0.0 74.7 jit_solution(11084031059806056997)
XLA Ops:
  0.0 74.1 %shard_map.73 = bf16[2,4,8192]{2,1,0:T(4,128)(2,1)S(1)} custom-call(bf16[2,4,8192]{2,1,0:T(4,128)(2,1)} %q_hbm.1, bf16[2,4,2048]{2,1,0:T(4,128)(2,1)} %fresh_hbm.1, s32[16,128]{1,0:T(8,128)} %bitcast.7, s32[16,128]{1,0:T(8,128)} %bitcast.8, s32[2,32]{1,0:T(2,128)} %bitcast.9, bf16[32,2,128,128]{3,2,1,0:T(8,128)(2,1)} %bitcast.5, ...), custom_call_target="tpu_custom_call" | custom-call | tf_op jit(solution)/shard_map/pallas_call | solution.py:380
  74.1 0.7 copy.9

commit v4 on v3

--- a/solution.py
+++ b/solution.py
@@ -56,6 +56,9 @@
             return n // nz, far - (i + 1) // 2 if i % 2 == 1 else far + i // 2
         return n // nz, jnp.where(i % 2 == 1, far - (i + 1) // 2, far + i // 2)
 
+    def place_of(z):
+        return jnp.where(z < far, 2 * (far - z) - 1, 2 * (z - far))
+
     def ahead(n):
         return at(*distance(n))
 
@@ -102,7 +105,11 @@
     def greet(s, h):
         pl.semaphore_signal(barrier, inc=1, device_id=(s, h), device_id_type=MESH)
 
-    for n in range(serve):
+    def hops(n):
+        y, z = distance(n)
+        return min(y, ny - y) + min(z, nz - z)
+
+    for n in sorted(range(serve), key=hops, reverse=True):
         if n != mine:
             greet(ahead(n), me_h)
     for i in range(1, heads):
@@ -150,8 +157,7 @@
         sent = jnp.where(half == lane, sub, sent)
         y = ((half >> 1) // nz - my_y) & (ny - 1)
         z = ((half >> 1) - my_z) & (nz - 1)
-        i = jnp.where(z < far, 2 * (far - z) - 1, 2 * (z - far))
-        places.append((y * nz + i) * 2 + (half & 1))
+        places.append((y * nz + place_of(z)) * 2 + (half & 1))
     table_v[0:host, :] = jnp.where(
         lane == 0, places[0], jnp.where(lane == 1, places[1], found & 255)
     )
@@ -284,27 +290,26 @@
                 send_lse(n)
 
         def send_some(q, k):
-            def one(n):
-                z = (my_z - distance(n)[1]) & (nz - 1)
-                quarter = jnp.minimum(z // (nz // 4), 2)
-
-                @pl.when((quarter == k) & (n != mine))
+            def one(i):
+                n = q * nz + place_of((my_z - i) & (nz - 1))
+
+                @pl.when(n != mine)
                 def _():
                     send_back(n)
 
-            fori(q * nz, q * nz + nz, one)
+            fori(k * (nz // 4), (k + 1) * (nz // 4), one)
 
         fori(first, first + nz, lse_other)
-        for k in range(3):
-
-            @pl.when(r >= k)
-            def _(k=k):
-                send_some(r - k, k)
+        for k, late in enumerate((0, 1, 2, 1)):
+
+            @pl.when(r >= late)
+            def _(k=k, late=late):
+                send_some(r - late, k)
 
         @pl.when(r == ny - 1)
         def _():
-            for k in range(3):
-                fori(ny - k, ny, lambda q, k=k: send_some(q, k))
+            for k, late in enumerate((0, 1, 2, 1)):
+                fori(ny - late, ny, lambda q, k=k: send_some(q, k))
 
     fori(0, ny, group)
     oin[mine] = osend[mine]

time: 74.8 us -> 74.4 us (level)
  no operation moved by 1% of the time
where the time goes in v4:
time: 74.4 us; the launch traced here: 74.3 us
  Pallas kernels  73.7 us (99%)
    pallas_call x1, Pallas kernels, local(): pl.pallas_call(functools.partial(kernel, cfg), out_shape=pltpu.VMEM(queri...  73.7 us

profile of v4, /device:TPU:1, one launch (start us, length us, event | category | flops | bytes accessed | tf_op | source)
XLA Modules:
  0.0 74.3 jit_solution(13334580076350524816)
XLA Ops:
  0.0 73.7 %shard_map.73 = bf16[2,4,8192]{2,1,0:T(4,128)(2,1)S(1)} custom-call(bf16[2,4,8192]{2,1,0:T(4,128)(2,1)} %q_hbm.1, bf16[2,4,2048]{2,1,0:T(4,128)(2,1)} %fresh_hbm.1, s32[16,128]{1,0:T(8,128)} %bitcast.7, s32[16,128]{1,0:T(8,128)} %bitcast.8, s32[2,32]{1,0:T(2,128)} %bitcast.9, bf16[32,2,128,128]{3,2,1,0:T(8,128)(2,1)} %bitcast.5, ...), custom_call_target="tpu_custom_call" | custom-call | tf_op jit(solution)/shard_map/pallas_call | solution.py:385
  73.7 0.7 copy.9

commit v5 on v4

--- a/solution.py
+++ b/solution.py
@@ -300,7 +300,7 @@
             fori(k * (nz // 4), (k + 1) * (nz // 4), one)
 
         fori(first, first + nz, lse_other)
-        for k, late in enumerate((0, 1, 2, 1)):
+        for k, late in enumerate((0, 1, 3, 1)):
 
             @pl.when(r >= late)
             def _(k=k, late=late):
@@ -308,7 +308,7 @@
 
         @pl.when(r == ny - 1)
         def _():
-            for k, late in enumerate((0, 1, 2, 1)):
+            for k, late in enumerate((0, 1, 3, 1)):
                 fori(ny - late, ny, lambda q, k=k: send_some(q, k))
 
     fori(0, ny, group)

time: 74.4 us -> 75 us (level); the launches traced: 74.3 us -> 74.1 us
  no operation moved by 1% of the time
where the time goes in v5:
time: 75 us; the launch traced here: 74.1 us
  Pallas kernels  73.4 us (98%)
    pallas_call x1, Pallas kernels, local(): pl.pallas_call(functools.partial(kernel, cfg), out_shape=pltpu.VMEM(queri...  73.4 us

profile of v5, /device:TPU:1, one launch (start us, length us, event | category | flops | bytes accessed | tf_op | source)
XLA Modules:
  0.0 74.1 jit_solution(2375335936370267280)
XLA Ops:
  0.0 73.4 %shard_map.73 = bf16[2,4,8192]{2,1,0:T(4,128)(2,1)S(1)} custom-call(bf16[2,4,8192]{2,1,0:T(4,128)(2,1)} %q_hbm.1, bf16[2,4,2048]{2,1,0:T(4,128)(2,1)} %fresh_hbm.1, s32[16,128]{1,0:T(8,128)} %bitcast.7, s32[16,128]{1,0:T(8,128)} %bitcast.8, s32[2,32]{1,0:T(2,128)} %bitcast.9, bf16[32,2,128,128]{3,2,1,0:T(8,128)(2,1)} %bitcast.5, ...), custom_call_target="tpu_custom_call" | custom-call | tf_op jit(solution)/shard_map/pallas_call | solution.py:385
  73.4 0.7 copy.9
